TPU v7x, 512 devices: a whole 4x8x8 slice. The times are simulated.
512 devices in a mesh: attn: 16 (over z, x_hi), exp: 32 (over x_lo, y, core).
Axes of the slice: x: 4 (x_hi: 2, x_lo: 2; x = x_hi * 2 + x_lo), y: 8, z: 8, core: 2. Of those that a mesh axis runs over, the one named last changes fastest.
Arguments:
- residual: bfloat16 [4096, 2880], P(('exp', 'attn')), may hold values from -16 to 16
- queries: bfloat16 [4096, 2048], P(('exp', 'attn')), may hold values from -6 to 6
- window_key_value_cache: bfloat16 [4096, 4, 128, 128], P(('exp', 'attn')), may hold values from -6 to 6
- new_key_value: bfloat16 [4096, 4, 128], P(('exp', 'attn')), may hold values from -5.5 to 5.5
- head_sink_logits: float32 [32], replicated, may hold values from 0 to 5
- out_proj: bfloat16 [2048, 2880], P('attn'), may hold values from -0.125 to 0.125
- norm_gain: float32 [2880], replicated, may hold values from 0.5 to 1.5
- expert_ids: int32 [4096, 4], P('exp'), may hold values from 0 to 31, as said below
- gate_mix: float32 [4096, 4], P('exp'), may hold values from 0.05 to 0.6
- w_gate: bfloat16 [32, 2880, 2880], P('exp', None, 'attn'), may hold values from -0.109375 to 0.109375
- w_up: bfloat16 [32, 2880, 2880], P('exp', None, 'attn'), may hold values from -0.109375 to 0.109375
- w_down: bfloat16 [32, 2880, 2880], P('exp', 'attn'), may hold values from -0.109375 to 0.109375
Outputs:
- layer_out: bfloat16 [4096, 2880], P(('exp', 'attn'))
Inputs may be any that keep to these rules, and one draw needn't show every extreme that they name: `expert_ids`: each row names 4 different experts. Within the rows of one index of exp (aligned blocks of 128 rows) no expert is named more than 32 times, and one expert is named exactly 32 times in every block.
All inputs are finite; a program needn't handle non-finite values.
Results may differ from a plain program's by a relative error of at most 0.02.
Values may be sent and summed in bfloat16 or wider, within the bound.
No kernel may reach another device: no remote copies, remote signals or barrier semaphores. Data moves between devices by JAX's collectives and lax.ppermute only.
A program may use at most 128 MiB of HBM per device.

v0:
```python
import jax
import jax.numpy as jnp
from jax import lax
from jax.sharding import PartitionSpec as P

HEAD_SIZE = 64
QUERY_HEADS = 32
KEY_VALUE_HEADS = 4


def attend(queries, window_key_value_cache, new_key_value, head_sink_logits):
    count_of_rows = queries.shape[0]
    query_groups = QUERY_HEADS // KEY_VALUE_HEADS
    grouped_queries = queries.reshape(count_of_rows, KEY_VALUE_HEADS, query_groups, HEAD_SIZE)
    all_keys = jnp.concatenate(
        [window_key_value_cache[:, :, :, :HEAD_SIZE], new_key_value[:, :, None, :HEAD_SIZE]], axis=2
    )
    all_values = jnp.concatenate(
        [window_key_value_cache[:, :, :, HEAD_SIZE:], new_key_value[:, :, None, HEAD_SIZE:]], axis=2
    )
    scores = jnp.einsum(
        "rkgd,rkjd->rkgj", grouped_queries, all_keys, preferred_element_type=jnp.float32
    ) * HEAD_SIZE ** (-0.5)
    sink_portion = head_sink_logits.reshape(1, KEY_VALUE_HEADS, query_groups, 1)
    highest = jnp.maximum(jnp.max(scores, axis=3, keepdims=True), sink_portion)
    raised = jnp.exp(scores - highest)
    denominator = jnp.sum(raised, axis=3, keepdims=True) + jnp.exp(sink_portion - highest)
    weights = (raised / denominator).astype(jnp.bfloat16)
    combined = jnp.einsum(
        "rkgj,rkjd->rkgd", weights, all_values, preferred_element_type=jnp.float32
    )
    return combined.reshape(count_of_rows, QUERY_HEADS * HEAD_SIZE).astype(jnp.bfloat16)


def run_experts(row_block, w_gate, w_up, w_down):
    sources, slot_count, width = row_block.shape
    local_experts = w_gate.shape[0]
    grouped_queries = row_block.reshape(sources // local_experts, local_experts, slot_count, width)
    gate_proj = jnp.einsum(
        "sjcd,jdf->sjcf", grouped_queries, w_gate, preferred_element_type=jnp.float32
    )
    up_proj = jnp.einsum(
        "sjcd,jdf->sjcf", grouped_queries, w_up, preferred_element_type=jnp.float32
    )
    activated = (gate_proj * jax.nn.sigmoid(1.702 * gate_proj) * (up_proj + 1.0)).astype(
        jnp.bfloat16
    )
    partial_value = jnp.einsum(
        "sjcf,jfd->sjcd", activated, w_down, preferred_element_type=jnp.float32
    ).astype(jnp.bfloat16)
    return partial_value.reshape(sources, slot_count, width)


def local(
    residual,
    queries,
    window_key_value_cache,
    new_key_value,
    head_sink_logits,
    out_proj,
    norm_gain,
    expert_ids,
    gate_mix,
    w_gate,
    w_up,
    w_down,
):
    column_rows, top_count = expert_ids.shape
    expert_total = w_gate.shape[0] * lax.axis_size("exp")
    capacity = 2 * column_rows * top_count // expert_total
    attention_output = attend(queries, window_key_value_cache, new_key_value, head_sink_logits)
    head_slices = lax.all_to_all(attention_output, "attn", split_axis=1, concat_axis=0, tiled=True)
    hidden_state = residual.astype(jnp.float32) + lax.psum_scatter(
        jnp.dot(head_slices, out_proj, preferred_element_type=jnp.float32).astype(jnp.bfloat16),
        "attn",
        scatter_dimension=0,
        tiled=True,
    ).astype(jnp.float32)
    mean_square = jnp.mean(hidden_state * hidden_state, axis=1, keepdims=True)
    normed = (hidden_state * lax.rsqrt(mean_square + 1e-05) * norm_gain).astype(jnp.bfloat16)
    flat_ids = expert_ids.reshape(-1)
    onehot_table = (flat_ids[:, None] == jnp.arange(expert_total, dtype=jnp.int32)[None, :]).astype(
        jnp.int32
    )
    slot_index = jnp.sum((jnp.cumsum(onehot_table, axis=0) - 1) * onehot_table, axis=1)
    places = flat_ids * capacity + slot_index
    row_number = jnp.arange(column_rows * top_count, dtype=jnp.int32) // top_count
    source_rows = (
        jnp.full((expert_total * capacity,), column_rows, jnp.int32).at[places].set(row_number)
    )
    column = lax.all_gather(normed, "attn", axis=0, tiled=True)
    padded = jnp.concatenate([column, jnp.zeros((1, column.shape[1]), jnp.bfloat16)], axis=0)
    outgoing = jnp.take(padded, source_rows, axis=0).reshape(
        expert_total, capacity, column.shape[1]
    )
    partial_value = run_experts(
        lax.all_to_all(outgoing, "exp", split_axis=0, concat_axis=0, tiled=True),
        w_gate,
        w_up,
        w_down,
    )
    returned = lax.all_to_all(partial_value, "exp", split_axis=0, concat_axis=0, tiled=True)
    picked = jnp.take(returned.reshape(expert_total * capacity, returned.shape[2]), places, axis=0)
    weighted = jnp.sum(
        picked.reshape(column_rows, top_count, picked.shape[1]).astype(jnp.float32)
        * gate_mix[:, :, None],
        axis=1,
    )
    combined = lax.psum_scatter(
        weighted.astype(jnp.bfloat16), "attn", scatter_dimension=0, tiled=True
    ).astype(jnp.float32)
    return (hidden_state + combined).astype(jnp.bfloat16)


def solution(mesh):
    in_specs = (
        P(("exp", "attn"), None),
        P(("exp", "attn"), None),
        P(("exp", "attn"), None, None, None),
        P(("exp", "attn"), None, None),
        P(),
        P("attn", None),
        P(),
        P("exp", None),
        P("exp", None),
        P("exp", None, "attn"),
        P("exp", None, "attn"),
        P("exp", "attn", None),
    )
    out_specs = P(("exp", "attn"), None)
    return jax.shard_map(local, mesh=mesh, in_specs=in_specs, out_specs=out_specs, check_vma=False)
```

profile of v0, /device:TPU:8, one launch (start us, length us, event | category | flops | bytes accessed | tf_op | source)
XLA Modules:
  0.0 752.3 jit_solution(5121819863465048144)
XLA Ops:
  8.5 2.2 fusion.41
  10.7 1.2 copy.55
  12.9 1.6 fusion.43
  15.9 12.9 %all-to-all-start = ((bf16[8,16,128]{2,0,1:T(8,128)(2,1)}), bf16[8,16,128]{2,0,1:T(8,128)(2,1)S(1)}, u32[]{:S(2)}, u32[]{:S(2)}) async-start(bf16[8,16,128]{2,0,1:T(8,128)(2,1)} %copy.47), calls=%async_computation | async-start | bytes 65536 | tf_op jit(solution)/shard_map/all_to_all | solution.py:72
  29.3 1.2 reduce-window.6
  31.0 8.1 %all-to-all-done = bf16[8,16,128]{2,0,1:T(8,128)(2,1)S(1)} async-done(((bf16[8,16,128]{2,0,1:T(8,128)(2,1)}), bf16[8,16,128]{2,0,1:T(8,128)(2,1)S(1)}, u32[]{:S(2)}, u32[]{:S(2)}) %all-to-all-start) | async-done | bytes 32800 | tf_op jit(solution)/shard_map/all_to_all | solution.py:72
  39.1 1.2 convolution_convert_fusion.1
  40.4 2.4 scatter_custom_fusion
  43.0 1.3 dynamic-slice
  44.9 154.8 %all-reduce.6.cloned.1.call-done = bf16[128,2880]{1,0:T(8,128)(2,1)} async-done(((bf16[128,2880]{1,0:T(8,128)(2,1)}), bf16[128,2880]{1,0:T(8,128)(2,1)}) %all-reduce.6.cloned.1.call-update) | async-done | bytes 737296
  201.5 44.4 %all_gather.3 = bf16[128,2880]{1,0:T(8,128)(2,1)S(1)} all-gather(bf16[8,2880]{1,0:T(8,128)(2,1)S(1)} %multiply_convert_fusion), channel_id=1, replica_groups=mesh['attn'=16,'exp'=32] {'attn'}, dimensions={0}, use_global_device_ids=true | all-gather | bytes 783360 | tf_op jit(solution)/shard_map/all_gather | solution.py:91
  246.0 6.5 gather_fusion
  252.6 3.4 broadcast_select_fusion
  256.0 143.5 %all_to_all.26 = bf16[32,32,2880]{2,1,0:T(8,128)(2,1)S(1)} all-to-all(bf16[32,32,2880]{2,1,0:T(8,128)(2,1)S(1)} %broadcast_select_fusion), channel_id=1, replica_groups=mesh['attn'=16,'exp'=32] {'exp'}, dimensions={0} | all-to-all | bytes 11796480 | tf_op jit(solution)/shard_map/all_to_all | solution.py:97
  399.5 2.6 copy-done.1
  402.1 2.8 convolution_bitcast_fusion
  404.9 12.4 %convolution_convert_fusion = bf16[32,32,2880]{2,1,0:T(8,128)(2,1)} fusion(bf16[32,32,2880]{2,1,0:T(8,128)(2,1)} %copy-done.1, bf16[1,180,2880]{2,1,0:T(8,128)(2,1)S(1)} %copy-done, bf16[1,2880,180]{1,2,0:T(8,128)(2,1)} %param.22, f32[32,1,32,180]{3,2,0,1:T(8,128)} %convolution_bitcast_fusion), kind=kOutput, calls=%fused_computation.5 | convolution fusion | flops 2127790080 | bytes 14607360 | tf_op jit(solution)/shard_map/sjcf,jfd->sjcd/dot_general | solution.py:48
  417.3 4.9 all-to-all-start.2
  422.9 132.2 %all-to-all-done.2 = bf16[32,32,2880]{2,1,0:T(8,128)(2,1)} async-done(((bf16[32,32,2880]{2,1,0:T(8,128)(2,1)}), bf16[32,32,2880]{2,1,0:T(8,128)(2,1)}, u32[]{:S(2)}, u32[]{:S(2)}) %all-to-all-start.2) | async-done | bytes 5898272 | tf_op jit(solution)/shard_map/all_to_all | solution.py:102
  555.1 10.2 %gather_fusion.1 = bf16[512,2880]{1,0:T(8,128)(2,1)} fusion(bf16[1024,2880]{1,0:T(8,128)(2,1)} %bitcast.24, s32[1024]{0:T(1024)S(1)} %pad_clamp_fusion), kind=kCustom, calls=%fused_computation.1 | custom fusion | bytes 5900288 | tf_op jit(solution)/shard_map/jit(_take)/gather | solution.py:103
  565.3 5.8 gather.15
  571.1 9.3 %multiply_reduce_fusion = bf16[128,2880]{1,0:T(8,128)(2,1)} fusion(f32[128,4]{1,0:T(8,128)S(1)} %copy.54, bf16[128,4,2880]{2,1,0:T(4,128)(2,1)} %gather.15, pred[128,4]{1,0:T(8,128)(4,1)S(1)} %copy.52), kind=kLoop, calls=%fused_computation.3 | loop fusion | flops 5529600 | bytes 3688960 | tf_op jit(solution)/shard_map/reduce_sum | solution.py:104
  580.5 163.5 %all-reduce.8.cloned.1.call-done = bf16[128,2880]{1,0:T(8,128)(2,1)} async-done(((bf16[128,2880]{1,0:T(8,128)(2,1)}), bf16[128,2880]{1,0:T(8,128)(2,1)}) %all-reduce.8.cloned.1.call-update) | async-done | bytes 737296
  744.0 1.5 add_convert_fusion
  (64 shorter events, 8.1 us)
Async XLA Ops:
  6.5 398.4 %copy-start = (bf16[1,180,2880]{2,1,0:T(8,128)(2,1)S(1)}, bf16[1,180,2880]{2,1,0:T(8,128)(2,1)}, u32[]{:S(2)}) copy-start(bf16[1,180,2880]{2,1,0:T(8,128)(2,1)} %param.23) | copy-start | bytes 3110404
  8.5 3.4 copy-start.4
  8.5 3.5 copy-start.8
  12.8 16.0 %copy-start.5 = (s32[128,4]{0,1:T(4,128)S(1)}, s32[128,4]{0,1:T(4,128)}, u32[]{:S(2)}) copy-start(s32[128,4]{0,1:T(4,128)} %param.19) | copy-start | bytes 6148
  12.9 26.3 %copy-start.2 = (bf16[128,2880]{0,1:T(8,128)(2,1)S(1)}, bf16[128,2880]{0,1:T(8,128)(2,1)}, u32[]{:S(2)}) copy-start(bf16[128,2880]{0,1:T(8,128)(2,1)} %param.17) | copy-start | bytes 2211844
  14.7 184.9 %copy-start.3 = (bf16[8,2880]{1,0:T(8,128)(2,1)S(1)}, bf16[8,2880]{1,0:T(8,128)(2,1)}, u32[]{:S(2)}) copy-start(bf16[8,2880]{1,0:T(8,128)(2,1)} %param.12) | copy-start | bytes 138244
  14.8 185.9 %copy-start.6 = (f32[2880]{0:T(1024)S(1)}, f32[2880]{0:T(1024)}, u32[]{:S(2)}) copy-start(f32[2880]{0:T(1024)} %param.18) | copy-start | bytes 34564
  15.9 23.2 %all-to-all-start = ((bf16[8,16,128]{2,0,1:T(8,128)(2,1)}), bf16[8,16,128]{2,0,1:T(8,128)(2,1)S(1)}, u32[]{:S(2)}, u32[]{:S(2)}) async-start(bf16[8,16,128]{2,0,1:T(8,128)(2,1)} %copy.47), calls=%async_computation | async-start | bytes 65536 | tf_op jit(solution)/shard_map/all_to_all | solution.py:72
  28.8 170.8 %all-reduce.6.cloned.1.call-start = ((), (), s32[]{:S(2)}) async-start(), calls=%async_computation.3 | async-start | bytes 1507328
  256.0 146.1 %copy-start.9 = (bf16[1,2880,180]{1,2,0:T(8,128)(2,1)S(1)}, bf16[1,2880,180]{1,2,0:T(8,128)(2,1)}, u32[]{:S(2)}) copy-start(bf16[1,2880,180]{1,2,0:T(8,128)(2,1)} %param.21) | copy-start | bytes 3110404
  399.5 2.6 copy-start.1
  417.3 5.5 copy-start.7
  417.3 137.8 %all-to-all-start.2 = ((bf16[32,32,2880]{2,1,0:T(8,128)(2,1)}), bf16[32,32,2880]{2,1,0:T(8,128)(2,1)}, u32[]{:S(2)}, u32[]{:S(2)}) async-start(bf16[32,32,2880]{2,1,0:T(8,128)(2,1)} %convolution_convert_fusion), calls=%async_computation.2 | async-start | bytes 12058624 | tf_op jit(solution)/shard_map/all_to_all | solution.py:102
  422.2 321.8 %all-reduce.8.cloned.1.call-start = ((), (), s32[]{:S(2)}) async-start(), calls=%async_computation.4 | async-start | bytes 1507328
Sparse Core Ops, SparseCore 0:
  40.5 159.1 all-reduce.5
  580.6 163.3 all-reduce.7
where the time goes:
time: 753 us; the launch traced here: 752 us
  waiting for transfers between devices  459 us (61%)
  blocking collectives  188 us (25%)
  local copies, waits for them, and re-layouts  37.3 us (5%)
  matrix products  18.5 us (2%)
  starting transfers between devices  18.1 us (2%)
  other arithmetic  17.6 us (2%)
  between operations  14.3 us (2%)
    unnamed x4, waiting for transfers between devices  318 us
    all_to_all x1, blocking collectives, local(): lax.all_to_all(outgoing, 'exp', split_axis=0, concat_axis=0, tiled=True)  144 us
    all_to_all x1, waiting for transfers between devices, local(): lax.all_to_all(partial_value, 'exp', split_axis=0, concat_axis=0, tiled=T...  132 us
    all_gather x1, blocking collectives, local(): column = lax.all_gather(normed, 'attn', axis=0, tiled=True)  44.4 us
    gather x2, local copies, waits for them, and re-layouts, local(): jnp.take(returned.reshape(expert_total * capacity, returned.shape[2]), pl...  16 us
  transfers between devices with their start and end apart: 4, of which 4 were waited for; matrix products, arithmetic and copies ran while one was open for 1% of the time, Pallas kernels for 0%

commit v1 on v0

--- a/solution.py
+++ b/solution.py
@@ -88,7 +88,9 @@
     source_rows = (
         jnp.full((expert_total * capacity,), column_rows, jnp.int32).at[places].set(row_number)
     )
-    column = lax.all_gather(normed, "attn", axis=0, tiled=True)
+    column = jnp.concatenate(
+        lax.all_to_all(jnp.stack([normed] * lax.psum(1, "attn"), axis=0), "attn", 0, 0), axis=0
+    )
     padded = jnp.concatenate([column, jnp.zeros((1, column.shape[1]), jnp.bfloat16)], axis=0)
     outgoing = jnp.take(padded, source_rows, axis=0).reshape(
         expert_total, capacity, column.shape[1]

time: 753 us -> 730 us (0.969)
  blocking collectives: 188 us -> 166 us
    all_gather x1 -> x0, blocking collectives: 44.4 us -> none  [local(): column = lax.all_gather(normed, 'attn', axis=0, tiled=True)]
    all_to_all x0 -> x1, blocking collectives: none -> 23 us  [local(): lax.all_to_all(attention_output, 'attn', split_axis=1, concat_axis=0, til...]
where the time goes in v1:
time: 730 us; the launch traced here: 729 us
  waiting for transfers between devices  464 us (64%)
  blocking collectives  166 us (23%)
  local copies, waits for them, and re-layouts  37.6 us (5%)
  matrix products  18.2 us (2%)
  other arithmetic  17.6 us (2%)
  between operations  14.3 us (2%)
  starting transfers between devices  11.6 us (2%)
    unnamed x4, waiting for transfers between devices  319 us
    all_to_all x1, blocking collectives, local(): lax.all_to_all(outgoing, 'exp', split_axis=0, concat_axis=0, tiled=True)  143 us
    all_to_all x1, waiting for transfers between devices, local(): lax.all_to_all(partial_value, 'exp', split_axis=0, concat_axis=0, tiled=T...  132 us
    all_to_all x1, blocking collectives, local(): lax.all_to_all(attention_output, 'attn', split_axis=1, concat_axis=0, til...  23 us
    gather x2, local copies, waits for them, and re-layouts, local(): jnp.take(returned.reshape(expert_total * capacity, returned.shape[2]), pl...  16 us
  transfers between devices with their start and end apart: 4, of which 4 were waited for; matrix products, arithmetic and copies ran while one was open for 1% of the time, Pallas kernels for 0%

profile of v1, /device:TPU:8, one launch (start us, length us, event | category | flops | bytes accessed | tf_op | source)
XLA Modules:
  0.0 729.2 jit_solution(6351002878392564112)
XLA Ops:
  8.5 2.2 fusion.41
  10.7 1.2 copy.55
  12.9 1.6 fusion.43
  15.3 23.0 %all_to_all.31 = bf16[8,16,128]{2,0,1:T(8,128)(2,1)S(1)} all-to-all(bf16[8,16,128]{2,0,1:T(8,128)(2,1)S(1)} %copy.47), channel_id=1, replica_groups=mesh['attn'=16,'exp'=32] {'attn'}, dimensions={1} | all-to-all | bytes 65536 | tf_op jit(solution)/shard_map/all_to_all | solution.py:72
  38.3 1.2 convolution_convert_fusion.1
  39.9 1.3 dynamic-slice
  41.8 156.9 %all-reduce.6.cloned.1.call-done = bf16[128,2880]{1,0:T(8,128)(2,1)} async-done(((bf16[128,2880]{1,0:T(8,128)(2,1)}), bf16[128,2880]{1,0:T(8,128)(2,1)}) %all-reduce.6.cloned.1.call-update) | async-done | bytes 737296
  201.5 6.4 all-to-all-start.1
  208.0 1.2 reduce-window.6
  209.7 2.4 scatter_custom_fusion
  212.3 12.8 %all-to-all-done.1 = bf16[16,8,2880]{2,1,0:T(8,128)(2,1)S(1)} async-done(((bf16[16,8,2880]{2,1,0:T(8,128)(2,1)}), bf16[16,8,2880]{2,1,0:T(8,128)(2,1)S(1)}, u32[]{:S(2)}, u32[]{:S(2)}) %all-to-all-start.1) | async-done | bytes 737312 | tf_op jit(solution)/shard_map/all_to_all | solution.py:92
  225.2 6.5 gather_fusion
  231.7 3.4 broadcast_select_fusion
  235.1 143.1 %all_to_all.32 = bf16[32,32,2880]{2,1,0:T(8,128)(2,1)S(1)} all-to-all(bf16[32,32,2880]{2,1,0:T(8,128)(2,1)S(1)} %broadcast_select_fusion), channel_id=1, replica_groups=mesh['attn'=16,'exp'=32] {'exp'}, dimensions={0} | all-to-all | bytes 11796480 | tf_op jit(solution)/shard_map/all_to_all | solution.py:99
  378.2 2.6 copy-done.1
  380.8 2.8 convolution_bitcast_fusion
  383.6 12.1 %convolution_convert_fusion = bf16[32,32,2880]{2,1,0:T(8,128)(2,1)} fusion(bf16[32,32,2880]{2,1,0:T(8,128)(2,1)} %copy-done.1, bf16[1,180,2880]{2,1,0:T(8,128)(2,1)S(1)} %copy-done, bf16[1,2880,180]{1,2,0:T(8,128)(2,1)S(1)} %copy-done.10, f32[32,1,32,180]{3,2,0,1:T(8,128)} %convolution_bitcast_fusion), kind=kOutput, calls=%fused_computation.5 | convolution fusion | flops 2127790080 | bytes 14607360 | tf_op jit(solution)/shard_map/sjcf,jfd->sjcd/dot_general | solution.py:48
  395.7 4.9 all-to-all-start.3
  401.4 132.2 %all-to-all-done.3 = bf16[32,32,2880]{2,1,0:T(8,128)(2,1)} async-done(((bf16[32,32,2880]{2,1,0:T(8,128)(2,1)}), bf16[32,32,2880]{2,1,0:T(8,128)(2,1)}, u32[]{:S(2)}, u32[]{:S(2)}) %all-to-all-start.3) | async-done | bytes 5898272 | tf_op jit(solution)/shard_map/all_to_all | solution.py:104
  533.5 10.2 %gather_fusion.1 = bf16[512,2880]{1,0:T(8,128)(2,1)} fusion(bf16[1024,2880]{1,0:T(8,128)(2,1)} %bitcast.25, s32[1024]{0:T(1024)S(1)} %pad_clamp_fusion), kind=kCustom, calls=%fused_computation.1 | custom fusion | bytes 5900288 | tf_op jit(solution)/shard_map/jit(_take)/gather | solution.py:105
  543.7 5.8 gather.15
  549.6 9.3 %multiply_reduce_fusion = bf16[128,2880]{1,0:T(8,128)(2,1)} fusion(f32[128,4]{1,0:T(8,128)S(1)} %copy.54, bf16[128,4,2880]{2,1,0:T(4,128)(2,1)} %gather.15, pred[128,4]{1,0:T(8,128)(4,1)S(1)} %copy.52), kind=kLoop, calls=%fused_computation.3 | loop fusion | flops 5529600 | bytes 3688960 | tf_op jit(solution)/shard_map/reduce_sum | solution.py:106
  558.9 162.0 %all-reduce.8.cloned.1.call-done = bf16[128,2880]{1,0:T(8,128)(2,1)} async-done(((bf16[128,2880]{1,0:T(8,128)(2,1)}), bf16[128,2880]{1,0:T(8,128)(2,1)}) %all-reduce.8.cloned.1.call-update) | async-done | bytes 737296
  720.9 1.5 add_convert_fusion
  (67 shorter events, 8.3 us)
Async XLA Ops:
  6.5 377.1 %copy-start = (bf16[1,180,2880]{2,1,0:T(8,128)(2,1)S(1)}, bf16[1,180,2880]{2,1,0:T(8,128)(2,1)}, u32[]{:S(2)}) copy-start(bf16[1,180,2880]{2,1,0:T(8,128)(2,1)} %param.23) | copy-start | bytes 3110404
  6.5 192.2 %all-reduce.6.cloned.1.call-start = ((), (), s32[]{:S(2)}) async-start(), calls=%async_computation.4 | async-start | bytes 1507328
  8.5 3.4 copy-start.4
  8.5 3.5 copy-start.8
  12.8 25.4 %copy-start.2 = (bf16[128,2880]{0,1:T(8,128)(2,1)S(1)}, bf16[128,2880]{0,1:T(8,128)(2,1)}, u32[]{:S(2)}) copy-start(bf16[128,2880]{0,1:T(8,128)(2,1)} %param.17) | copy-start | bytes 2211844
  14.5 25.1 %copy-start.5 = (s32[128,4]{0,1:T(4,128)S(1)}, s32[128,4]{0,1:T(4,128)}, u32[]{:S(2)}) copy-start(s32[128,4]{0,1:T(4,128)} %param.19) | copy-start | bytes 6148
  14.5 184.3 %copy-start.3 = (bf16[8,2880]{1,0:T(8,128)(2,1)S(1)}, bf16[8,2880]{1,0:T(8,128)(2,1)}, u32[]{:S(2)}) copy-start(bf16[8,2880]{1,0:T(8,128)(2,1)} %param.12) | copy-start | bytes 138244
  14.5 185.2 %copy-start.6 = (f32[2880]{0:T(1024)S(1)}, f32[2880]{0:T(1024)}, u32[]{:S(2)}) copy-start(f32[2880]{0:T(1024)} %param.18) | copy-start | bytes 34564
  201.5 23.6 %all-to-all-start.1 = ((bf16[16,8,2880]{2,1,0:T(8,128)(2,1)}), bf16[16,8,2880]{2,1,0:T(8,128)(2,1)S(1)}, u32[]{:S(2)}, u32[]{:S(2)}) async-start(bf16[16,8,2880]{2,1,0:T(8,128)(2,1)} %stack.2), calls=%async_computation.1 | async-start | bytes 1507328 | tf_op jit(solution)/shard_map/all_to_all | solution.py:92
  235.1 145.7 %copy-start.9 = (bf16[1,2880,180]{1,2,0:T(8,128)(2,1)S(1)}, bf16[1,2880,180]{1,2,0:T(8,128)(2,1)}, u32[]{:S(2)}) copy-start(bf16[1,2880,180]{1,2,0:T(8,128)(2,1)} %param.21) | copy-start | bytes 3110404
  378.2 2.6 copy-start.1
  380.8 2.8 copy-start.10
  395.7 5.5 copy-start.7
  395.7 137.8 %all-to-all-start.3 = ((bf16[32,32,2880]{2,1,0:T(8,128)(2,1)}), bf16[32,32,2880]{2,1,0:T(8,128)(2,1)}, u32[]{:S(2)}, u32[]{:S(2)}) async-start(bf16[32,32,2880]{2,1,0:T(8,128)(2,1)} %convolution_convert_fusion), calls=%async_computation.3 | async-start | bytes 12058624 | tf_op jit(solution)/shard_map/all_to_all | solution.py:104
  400.6 320.3 %all-reduce.8.cloned.1.call-start = ((), (), s32[]{:S(2)}) async-start(), calls=%async_computation.5 | async-start | bytes 1507328
Sparse Core Ops, SparseCore 0:
  39.7 159.0 all-reduce.5
  559.0 161.8 all-reduce.7
